TPU v7x, 32 devices: a whole 2x2x4 slice. The times are simulated.
32 devices in a mesh: zn: 2 (over x), zw: 16 (over z, y, core).
Axes of the slice: x: 2, y: 2, z: 4, core: 2. Of those that a mesh axis runs over, the one named last changes fastest.
Arguments:
- basis: float32 [64, 32, 8, 256], P(None, 'zw', None, 'zn'), may hold values from -360 to 360
- coupling: bfloat16 [27, 32, 8, 256], P(None, 'zw', None, 'zn'), may hold values from -0.099609375 to 0.099609375
Outputs:
- q_basis: float32 [64, 32, 8, 256], P(None, 'zw', None, 'zn')
- r_factor: float32 [64, 64], replicated
All inputs are finite; a program needn't handle non-finite values.
Results may differ from a plain program's by a relative error of at most 0.0003.
Values may be sent and summed in bfloat16 or wider, within the bound.
A program may use at most 64 MiB of HBM per device.

v0:
```python
import jax
import jax.numpy as jnp
from jax import lax
from jax.sharding import PartitionSpec as P


def with_halo(x, sides, width, wrap):
    for axis, dim in sides:
        size, length = (lax.axis_size(axis), x.shape[dim])
        up = [(i, (i + 1) % size) for i in range(size if wrap else size - 1)]
        down = [(j, i) for i, j in up]
        last = lax.slice_in_dim(x, length - width, length, axis=dim)
        initial = lax.slice_in_dim(x, 0, width, axis=dim)
        before = lax.ppermute(last, axis, up)
        after = lax.ppermute(initial, axis, down)
        x = jnp.concatenate([before, x, after], axis=dim)
    return x


def sweep(extended, coupling):
    planes_here = coupling.shape[1]
    span_here = coupling.shape[3]
    wrapped = jnp.concatenate([extended[:, :, -1:], extended, extended[:, :, :1]], axis=2)
    rows_x = extended.shape[2]
    summed = extended[:, 1 : planes_here + 1, :, 1 : span_here + 1]
    for shift_z in (-1, 0, 1):
        for shift_x in (-1, 0, 1):
            for shift_y in (-1, 0, 1):
                offset = 9 * (shift_z + 1) + 3 * (shift_x + 1) + shift_y + 1
                source = wrapped[
                    :,
                    1 + shift_z : 1 + shift_z + planes_here,
                    1 + shift_x : 1 + shift_x + rows_x,
                    1 + shift_y : 1 + shift_y + span_here,
                ]
                summed = summed + coupling[offset].astype(jnp.float32)[None] * source
    return summed


def inner_products(flat_basis):
    return jnp.dot(flat_basis, flat_basis.T, precision=lax.Precision.HIGHEST)


def upper_cholesky(gram_matrix):
    order = gram_matrix.shape[0]
    places = jnp.arange(order, dtype=jnp.int32)

    def one_row(index, upper):
        column = lax.dynamic_slice_in_dim(upper, index, 1, 1)[:, 0]
        target = lax.dynamic_slice_in_dim(gram_matrix, index, 1, 0)[0]
        remain = target - jnp.dot(column, upper, precision=lax.Precision.HIGHEST)
        pivot = jnp.sqrt(jnp.sum(jnp.where(places == index, remain, 0.0)))
        new_row = jnp.where(places > index, remain / pivot, jnp.where(places == index, pivot, 0.0))
        return lax.dynamic_update_slice_in_dim(upper, new_row[None], index, 0)

    return lax.fori_loop(0, order, one_row, jnp.zeros_like(gram_matrix))


def upper_inverse(upper):
    order = upper.shape[0]
    places = jnp.arange(order, dtype=jnp.int32)

    def one_row(step, inverse):
        index = order - 1 - step
        row = lax.dynamic_slice_in_dim(upper, index, 1, 0)[0]
        pivot = jnp.sum(jnp.where(places == index, row, 0.0))
        above = jnp.where(places > index, row, 0.0)
        unit = jnp.where(places == index, 1.0, 0.0).astype(upper.dtype)
        new_row = (unit - jnp.dot(above, inverse, precision=lax.Precision.HIGHEST)) / pivot
        return lax.dynamic_update_slice_in_dim(inverse, new_row[None], index, 0)

    return lax.fori_loop(0, order, one_row, jnp.zeros_like(upper))


def on_device(basis, coupling):
    field_now = basis
    for repeat in range(2):
        planes_wide = with_halo(field_now, (("zw", 1),), 1, False)
        extended = with_halo(planes_wide, (("zn", 3),), 1, True)
        field_now = sweep(extended, coupling)
    columns = field_now.shape[0]
    flat_basis = field_now.reshape(columns, -1)
    total_cells = flat_basis.shape[1] * lax.axis_size(("zn", "zw"))
    gram_matrix = lax.psum(inner_products(flat_basis), ("zn", "zw"))
    upper_factor = upper_cholesky(gram_matrix)
    inverse = upper_inverse(upper_factor)
    q_flat = jnp.dot(inverse.T, flat_basis, precision=lax.Precision.HIGHEST)
    scale_root = jnp.sqrt(jnp.float32(total_cells))
    q_basis = (q_flat * scale_root).reshape(field_now.shape)
    return (q_basis, upper_factor / scale_root)


def solution(mesh):
    placed = (P(None, "zw", None, "zn"), P(None, "zw", None, "zn"))
    return jax.shard_map(
        on_device,
        mesh=mesh,
        in_specs=placed,
        out_specs=(P(None, "zw", None, "zn"), P()),
        check_vma=False,
    )
```

profile of v0, /device:TPU:0, one launch (start us, length us, event | category | flops | bytes accessed | tf_op | source)
XLA Modules:
  0.0 341.1 jit_solution(12545918661050327513)
XLA Ops:
  0.6 1.4 copy.55
  2.1 2.4 collective-permute-start
  4.5 1.3 collective-permute-start.1
  5.8 0.9 bitcast_convert_fusion.26
  6.7 3.7 %collective-permute-done.1 = f32[64,1,8,128]{0,2,3,1:T(8,128)S(1)} collective-permute-done((f32[64,1,8,128]{0,2,3,1:T(8,128)S(1)}, f32[64,1,8,128]{0,2,3,1:T(8,128)S(1)}, u32[]{:S(2)}, u32[]{:S(2)}) %collective-permute-start.1) | collective-permute-done | bytes 262176 | tf_op jit(solution)/shard_map/ppermute | solution.py:15
  10.5 1.5 collective-permute-start.2
  12.5 0.8 bitcast_convert_fusion.25
  13.7 0.8 copy.65
  14.5 0.8 copy.66
  15.3 0.8 copy.67
  16.1 0.8 copy.68
  16.9 0.8 copy.69
  17.6 0.8 copy.71
  18.4 0.8 copy.72
  19.2 0.8 copy.73
  20.8 0.8 copy.75
  21.6 0.8 copy.76
  22.4 0.8 copy.77
  23.9 0.8 copy.79
  24.7 0.8 copy.81
  25.5 0.8 copy.82
  26.3 0.8 copy.56
  27.1 0.8 copy.57
  27.9 0.8 copy.58
  28.6 0.8 copy.59
  29.4 0.8 copy.61
  31.0 0.8 copy.83
  31.8 0.8 copy.84
  32.9 1.5 fusion.22
  34.6 1.0 fusion.21
  36.4 9.0 %fusion.53 = f32[64,2,8,128]{0,2,3,1:T(8,128)S(1)} fusion(f32[64,4,9,130]{0,2,3,1:T(8,128)S(1)} %fusion.21, f32[64,4,8,129]{0,2,3,1:T(8,128)S(1)} %get-tuple-element.276, f32[64,1,8,128]{0,2,3,1:T(8,128)S(1)} %collective-permute-done.1, f32[64,2,8,128]{0,2,3,1:T(8,128)S(1)} %copy.55, f32[64,4,8,129]{0,2,3,1:T(8,128)S(1)} %get-tuple-element.275, ...), kind=kLoop, calls=%fused_computation.108 | loop fusion | flops 7340032 | bytes 14376960 | tf_op jit(solution)/shard_map/add | solution.py:36
  45.5 9.9 %collective-permute-start.4 = (f32[64,1,8,128]{0,2,3,1:T(8,128)S(1)}, f32[64,1,8,128]{0,2,3,1:T(8,128)S(1)}, u32[]{:S(2)}, u32[]{:S(2)}) collective-permute-start(f32[64,1,8,128]{0,2,3,1:T(8,128)S(1)} %get-tuple-element.279), channel_id=1, source_target_pairs={{0,1},{1,2},{2,3},{3,4},{4,5},{5,6},{6,7},{7,8},{8,9},{9,10},{10,1... | collective-permute-start | bytes 786440 | tf_op jit(solution)/shard_map/ppermute | solution.py:14
  55.4 1.3 collective-permute-start.5
  56.8 4.8 %collective-permute-done.5 = f32[64,1,8,128]{0,2,3,1:T(8,128)S(1)} collective-permute-done((f32[64,1,8,128]{0,2,3,1:T(8,128)S(1)}, f32[64,1,8,128]{0,2,3,1:T(8,128)S(1)}, u32[]{:S(2)}, u32[]{:S(2)}) %collective-permute-start.5) | collective-permute-done | bytes 262176 | tf_op jit(solution)/shard_map/ppermute | solution.py:15
  61.7 1.5 collective-permute-start.6
  63.7 1.7 collective-permute-done.6
  65.4 1.5 collective-permute-done.7
  66.9 1.5 fusion.20
  68.9 1.0 fusion.19
  70.6 9.0 %fusion.24 = f32[64,2,8,128]{0,2,3,1:T(8,128)S(1)} fusion(f32[64,4,9,130]{0,2,3,1:T(8,128)S(1)} %fusion.19, f32[64,4,8,129]{0,2,3,1:T(8,128)S(1)} %get-tuple-element.272, f32[64,1,8,128]{0,2,3,1:T(8,128)S(1)} %collective-permute-done.5, f32[64,2,8,128]{0,2,3,1:T(8,128)S(1)} %fusion.53, f32[64,4,8,129]{0,2,3,1:T(8,128)S(1)} %get-tuple-element.271, ...), kind=kLoop, calls=%fused_computation.53 | loop fusion | flops 7340032 | bytes 14376960 | tf_op jit(solution)/shard_map/add | solution.py:36
  80.1 2.0 convolution_bitcast_fusion.2
  82.1 49.0 %psum.7 = f32[64,64]{1,0:T(8,128)S(1)} all-reduce(f32[64,64]{1,0:T(8,128)S(1)} %convolution_bitcast_fusion.2), channel_id=1, replica_groups=mesh['zn'=2,'zw'=16] {'zn','zw'}, use_global_device_ids=true, to_apply=%region_0.0 | all-reduce | flops 4096 | bytes 32768 | tf_op jit(solution)/shard_map/psum | solution.py:84
  131.2 115.6 %while.32 = (s32[]{:T(128)}, f32[64,64]{0,1:T(8,128)S(1)}, f32[64,64]{1,0:T(8,128)S(1)}, s32[]{:T(128)}, s32[]{:T(128)}) while((s32[]{:T(128)}, f32[64,64]{0,1:T(8,128)S(1)}, f32[64,64]{1,0:T(8,128)S(1)}, s32[]{:T(128)}, s32[]{:T(128)}) %tuple.115), condition=%wide.region_3.4_spmd.clone.clone, body=%wide.region_1.3_spmd.clone.clone.sunk | while | flops 49729 | bytes 37205 | solution.py:56
  247.4 92.0 %while.33 = (s32[]{:T(128)}, f32[64,64]{1,0:T(8,128)S(1)}, f32[64,64]{1,0:T(8,128)S(1)}, s32[]{:T(128)}, s32[]{:T(128)}, /*index=5*/s32[]{:T(128)}, s32[]{:T(128)}) while((s32[]{:T(128)}, f32[64,64]{1,0:T(8,128)S(1)}, f32[64,64]{1,0:T(8,128)S(1)}, s32[]{:T(128)}, s32[]{:T(128)}, /*index=5*/s32[]{:T(128)}, ...), condition=%wide.region_6.7_spmd.clone.clone, body=%wide.region_4.6_spmd.clone.clone.sunk | while | flops 49733 | bytes 35983 | solution.py:72
  248.1 0.8 fusion.103
  249.5 0.8 fusion.103
  250.9 0.8 fusion.103
  252.4 0.8 fusion.103
  253.8 0.8 fusion.103
  256.7 0.8 fusion.103
  258.1 0.8 fusion.103
  259.6 0.8 fusion.103
  261.0 0.8 fusion.103
  262.4 0.8 fusion.103
  263.9 0.8 fusion.103
  265.3 0.8 fusion.103
  266.7 0.8 fusion.103
  268.2 0.8 fusion.103
  269.6 0.8 fusion.103
  271.1 0.8 fusion.103
  272.5 0.8 fusion.103
  273.9 0.8 fusion.103
  275.4 0.8 fusion.103
  340.2 0.9 copy.93
  (549 shorter events, 152.9 us)
Async XLA Ops:
  2.1 4.6 %collective-permute-start = (f32[64,1,8,128]{0,2,3,1:T(8,128)S(1)}, f32[64,1,8,128]{0,2,3,1:T(8,128)S(1)}, u32[]{:S(2)}, u32[]{:S(2)}) collective-permute-start(f32[64,1,8,128]{0,2,3,1:T(8,128)S(1)} %get-tuple-element.281), channel_id=1, source_target_pairs={{0,1},{1,2},{2,3},{3,4},{4,5},{5,6},{6,7},{7,8},{8,9},{9,10},{10,1... | collective-permute-start | bytes 786440 | tf_op jit(solution)/shard_map/ppermute | solution.py:14
  4.5 5.9 %collective-permute-start.1 = (f32[64,1,8,128]{0,2,3,1:T(8,128)S(1)}, f32[64,1,8,128]{0,2,3,1:T(8,128)S(1)}, u32[]{:S(2)}, u32[]{:S(2)}) collective-permute-start(f32[64,1,8,128]{0,2,3,1:T(8,128)S(1)} %get-tuple-element.282), channel_id=1, source_target_pairs={{1,0},{2,1},{3,2},{4,3},{5,4},{6,5},{7,6},{8,7},{9,8},{10,9},{11,1... | collective-permute-start | bytes 786440 | tf_op jit(solution)/shard_map/ppermute | solution.py:15
  10.5 22.1 %collective-permute-start.2 = (f32[64,4,8,1]{0,2,3,1:T(8,128)S(1)}, f32[64,4,8,1]{0,2,3,1:T(8,128)S(1)}, u32[]{:S(2)}, u32[]{:S(2)}) collective-permute-start(f32[64,4,8,1]{0,2,3,1:T(8,128)S(1)} %get-tuple-element.277), channel_id=1, source_target_pairs={{0,16},{16,0},{1,17},{17,1},{2,18},{18,2},{3,19},{19,3},{4,20},{20... | collective-permute-start | bytes 24584 | tf_op jit(solution)/shard_map/ppermute | solution.py:14
  12.0 20.6 %collective-permute-start.3 = (f32[64,4,8,1]{0,2,3,1:T(8,128)S(1)}, f32[64,4,8,1]{0,2,3,1:T(8,128)S(1)}, u32[]{:S(2)}, u32[]{:S(2)}) collective-permute-start(f32[64,4,8,1]{0,2,3,1:T(8,128)S(1)} %get-tuple-element.278), channel_id=1, source_target_pairs={{16,0},{0,16},{17,1},{1,17},{18,2},{2,18},{19,3},{3,19},{20,4},{4,... | collective-permute-start | bytes 24584 | tf_op jit(solution)/shard_map/ppermute | solution.py:15
  34.4 1.2 copy-start
  34.4 1.2 copy-start.2
  34.4 1.2 copy-start.4
  34.4 1.2 copy-start.6
  34.4 1.2 copy-start.8
  34.5 1.2 copy-start.10
  34.5 1.2 copy-start.12
  34.5 1.2 copy-start.14
  34.5 1.3 copy-start.16
  34.5 1.3 copy-start.18
  34.5 1.3 copy-start.20
  34.5 1.4 copy-start.22
  34.5 1.4 copy-start.24
  34.5 1.4 copy-start.26
  34.5 1.4 copy-start.28
  34.6 1.5 copy-start.30
  34.6 1.5 copy-start.32
  34.6 1.5 copy-start.34
  34.6 1.6 copy-start.36
  34.6 1.6 copy-start.38
  34.6 1.6 copy-start.40
  34.6 1.7 copy-start.42
  34.6 1.7 copy-start.44
  34.6 1.7 copy-start.46
  45.5 11.4 %collective-permute-start.4 = (f32[64,1,8,128]{0,2,3,1:T(8,128)S(1)}, f32[64,1,8,128]{0,2,3,1:T(8,128)S(1)}, u32[]{:S(2)}, u32[]{:S(2)}) collective-permute-start(f32[64,1,8,128]{0,2,3,1:T(8,128)S(1)} %get-tuple-element.279), channel_id=1, source_target_pairs={{0,1},{1,2},{2,3},{3,4},{4,5},{5,6},{6,7},{7,8},{8,9},{9,10},{10,1... | collective-permute-start | bytes 786440 | tf_op jit(solution)/shard_map/ppermute | solution.py:14
  55.4 6.3 %collective-permute-start.5 = (f32[64,1,8,128]{0,2,3,1:T(8,128)S(1)}, f32[64,1,8,128]{0,2,3,1:T(8,128)S(1)}, u32[]{:S(2)}, u32[]{:S(2)}) collective-permute-start(f32[64,1,8,128]{0,2,3,1:T(8,128)S(1)} %get-tuple-element.280), channel_id=1, source_target_pairs={{1,0},{2,1},{3,2},{4,3},{5,4},{6,5},{7,6},{8,7},{9,8},{10,9},{11,1... | collective-permute-start | bytes 786440 | tf_op jit(solution)/shard_map/ppermute | solution.py:15
  61.7 3.7 %collective-permute-start.6 = (f32[64,4,8,1]{0,2,3,1:T(8,128)S(1)}, f32[64,4,8,1]{0,2,3,1:T(8,128)S(1)}, u32[]{:S(2)}, u32[]{:S(2)}) collective-permute-start(f32[64,4,8,1]{0,2,3,1:T(8,128)S(1)} %get-tuple-element.273), channel_id=1, source_target_pairs={{0,16},{16,0},{1,17},{17,1},{2,18},{18,2},{3,19},{19,3},{4,20},{20... | collective-permute-start | bytes 24584 | tf_op jit(solution)/shard_map/ppermute | solution.py:14
  63.2 3.7 %collective-permute-start.7 = (f32[64,4,8,1]{0,2,3,1:T(8,128)S(1)}, f32[64,4,8,1]{0,2,3,1:T(8,128)S(1)}, u32[]{:S(2)}, u32[]{:S(2)}) collective-permute-start(f32[64,4,8,1]{0,2,3,1:T(8,128)S(1)} %get-tuple-element.274), channel_id=1, source_target_pairs={{16,0},{0,16},{17,1},{1,17},{18,2},{2,18},{19,3},{3,19},{20,4},{4,... | collective-permute-start | bytes 24584 | tf_op jit(solution)/shard_map/ppermute | solution.py:15
  68.7 1.2 copy-start.1
  68.7 1.2 copy-start.3
  68.7 1.2 copy-start.5
  68.7 1.2 copy-start.7
  68.7 1.2 copy-start.9
  68.7 1.2 copy-start.11
  68.8 1.2 copy-start.13
  68.8 1.2 copy-start.15
  68.8 1.3 copy-start.17
  68.8 1.3 copy-start.19
  68.8 1.3 copy-start.21
  68.8 1.4 copy-start.23
  68.8 1.4 copy-start.25
  68.8 1.4 copy-start.27
  68.8 1.4 copy-start.29
  68.8 1.5 copy-start.31
  68.9 1.5 copy-start.33
  68.9 1.5 copy-start.35
  68.9 1.6 copy-start.37
  68.9 1.6 copy-start.39
  68.9 1.6 copy-start.41
  68.9 1.7 copy-start.43
  68.9 1.7 copy-start.45
  68.9 1.7 copy-start.47
where the time goes:
time: 344 us; the launch traced here: 341 us
  matrix products  102 us (30%)
  other arithmetic  65.1 us (19%)
  blocking collectives  49 us (14%)
  loops' own time  47.8 us (14%)
  local copies, waits for them, and re-layouts  44.8 us (13%)
  starting transfers between devices  18.9 us (5%)
  waiting for transfers between devices  11.9 us (3%)
    dot_general x64, matrix products, one_row(): jnp.dot(above, inverse, precision=lax.Precision.HIGHEST)  50 us
    dot_general x64, matrix products, one_row(): remain = target - jnp.dot(column, upper, precision=lax.Precision.HIGHEST)  49.4 us
    psum x1, blocking collectives, on_device(): gram_matrix = lax.psum(inner_products(flat_basis), ('zn', 'zw'))  49 us
    another operation x1, loops' own time, upper_cholesky(): return lax.fori_loop(0, order, one_row, jnp.zeros_like(gram_matrix))  46.3 us
    reduce_sum x64, other arithmetic, one_row(): pivot = jnp.sum(jnp.where(places == index, row, 0.0))  38.8 us
    mul x27, local copies, waits for them, and re-layouts, sweep(): summed = summed + coupling[offset].astype(jnp.float32)[None] * source  19.3 us
    add x2, other arithmetic, sweep(): summed = summed + coupling[offset].astype(jnp.float32)[None] * source  18.1 us
    ppermute x4, starting transfers between devices, with_halo(): before = lax.ppermute(last, axis, up)  15.2 us
  transfers between devices with their start and end apart: 8, of which 5 were waited for; matrix products, arithmetic and copies ran while one was open for 6% of the time, Pallas kernels for 0%

commit v1 on v0

v1 whole, which is shorter than its diff:
```python
import functools

import jax
import jax.numpy as jnp
from jax import lax
from jax.experimental import pallas as pl
from jax.experimental.pallas import tpu as pltpu
from jax.sharding import PartitionSpec as P

MESH = pl.DeviceIdType.MESH
CHUNKS = 4


def inner_size(n):
    s = 1
    while s * s < n:
        s *= 2
    while n % s:
        s //= 2
    return s


def kernel(
    n_zn, n_zw, cells, basis, coupling, q_out, r_out,
    f0, f1, x2, cpl, ysend, yrecv, xs, buf_a, buf_b,
    load_sem, z_send, z_recv, y_send, y_recv, a_send, a_recv, b_send, b_recv,
):
    zn = lax.axis_index("zn")
    zw = lax.axis_index("zw")
    has_lo = zw > 0
    has_hi = zw < n_zw - 1
    cols = basis.shape[0]
    per = cols // CHUNKS
    n_dir = yrecv.shape[0]
    si = inner_size(n_zw)
    so = n_zw // si
    n_a = n_zn * si
    sides = (1,) if n_dir == 1 else (1, n_zn - 1)

    def beside(step):
        return (zn + step) % n_zn

    inner = zw % si
    outer = zw // si
    me_a = zn * si + inner

    def partner_a(off):
        other = (me_a + off) % n_a
        return other, {"zn": other // si, "zw": outer * si + other % si}

    def partner_b(off):
        other = (outer + off) % so
        return other, {"zn": zn, "zw": other * si + inner}

    barrier = pltpu.get_barrier_semaphore()

    def greet(dev):
        pl.semaphore_signal(barrier, inc=1, device_id=dev, device_id_type=MESH)

    for present, dz in ((has_lo, -1), (has_hi, 1)):
        @pl.when(present)
        def _(dz=dz):
            greet({"zn": zn, "zw": zw + dz})
            for side in sides:
                greet({"zn": beside(side), "zw": zw + dz})
    for off in range(1, n_a):
        greet(partner_a(off)[1])
    for off in range(1, so):
        greet(partner_b(off)[1])

    loads = [
        pltpu.make_async_copy(basis.at[:, z], f0.at[1 + z], load_sem.at[z]) for z in range(2)
    ]
    for copy in loads:
        copy.start()

    lane = lax.broadcasted_iota(jnp.int32, (8, 128), 1)
    sub = lax.broadcasted_iota(jnp.int32, (8, 128), 0)
    pair = lane // 2
    zero_tile = jnp.zeros((8, 128), jnp.float32)

    for present, plane in ((has_lo, 0), (has_hi, 3)):
        @pl.when(jnp.logical_not(present))
        def _(plane=plane):
            f0[plane] = jnp.zeros(f0.shape[1:], jnp.float32)
            f1[plane] = jnp.zeros(f1.shape[1:], jnp.float32)
            for d in range(n_dir):
                for c in range(CHUNKS + 1):
                    yrecv[d, c, plane] = zero_tile

    total = (n_a - 1) + (so - 1)
    both = has_lo.astype(jnp.int32) + has_hi.astype(jnp.int32)
    pl.semaphore_wait(barrier, total + both * (1 + len(sides)))

    def z_copy(e, c, way):
        part = pl.ds(c * per, per)
        if e == 0:
            src = basis.at[part, way]
        else:
            src = f1.at[1 + way, part]
        dst = (f0, f1)[e].at[3 if way == 0 else 0, part]
        return pltpu.make_async_remote_copy(
            src_ref=src, dst_ref=dst,
            send_sem=z_send.at[e, c, way], recv_sem=z_recv.at[e, c, way],
            device_id={"zn": zn, "zw": zw + (-1 if way == 0 else 1)}, device_id_type=MESH,
        )

    def z_start(e, c):
        for way, present in ((0, has_lo), (1, has_hi)):
            @pl.when(present)
            def _(way=way):
                z_copy(e, c, way).start()

    def z_wait(e, c):
        for way, present in ((0, has_hi), (1, has_lo)):
            @pl.when(present)
            def _(way=way):
                z_copy(e, c, way).wait_recv()

    def y_copy(slot, d, which):
        dz, src, dst = ((0, (0, 2), 1), (-1, (0, 1), 3), (1, (1, 1), 0))[which]
        return pltpu.make_async_remote_copy(
            src_ref=ysend.at[slot, pl.ds(src[0], src[1])],
            dst_ref=yrecv.at[d, slot, pl.ds(dst, src[1])],
            send_sem=y_send.at[slot, d, which], recv_sem=y_recv.at[slot, d, which],
            device_id={"zn": beside(sides[d]), "zw": zw + dz}, device_id_type=MESH,
        )

    def y_start(slot):
        for d in range(n_dir):
            y_copy(slot, d, 0).start()
            for which, present in ((1, has_lo), (2, has_hi)):
                @pl.when(present)
                def _(d=d, which=which):
                    y_copy(slot, d, which).start()

    def y_wait(slot):
        for d in range(n_dir):
            y_copy(slot, d, 0).wait_recv()
            for which, present in ((1, has_hi), (2, has_lo)):
                @pl.when(present)
                def _(d=d, which=which):
                    y_copy(slot, d, which).wait_recv()

    for c in range(CHUNKS):
        z_start(0, c)

    for copy in loads:
        copy.wait()

    def pack_into(packed, tile, k):
        return jnp.where(pair == k, pltpu.roll(tile, 2 * k + 1, 1), packed)

    def pack_first(step, packs):
        packs = list(packs)
        for u in range(4):
            k = step * 4 + u
            for z in range(2):
                packs[z] = pack_into(packs[z], f0[1 + z, k], k)
        return tuple(packs)

    packs = lax.fori_loop(0, cols // 4, pack_first, (zero_tile, zero_tile))
    for z in range(2):
        ysend[0, z] = packs[z]
    y_start(0)

    for z in range(2):
        for b in range(3):
            for a in range(3):
                for c in range(3):
                    tile = coupling[9 * a + 3 * b + c, z].astype(jnp.float32)
                    if b != 1:
                        tile = pltpu.roll(tile, (b - 1) % 8, 0)
                    cpl[z, 9 * b + 3 * a + c] = tile

    def arrived(slot):
        result = []
        for plane in range(4):
            tile = yrecv[0, slot, plane]
            if n_dir == 2:
                tile = jnp.where(lane % 2 == 0, tile, yrecv[1, slot, plane])
            result.append(tile)
        return result

    def step_column(f, k, edges):
        shifted = []
        for plane in range(4):
            tile = f[plane, k]
            edge = pltpu.roll(edges[plane], 127 - 2 * k, 1)
            before = pltpu.roll(jnp.where(lane == 127, edge, tile), 1, 1)
            after = pltpu.roll(jnp.where(lane == 0, edge, tile), 127, 1)
            shifted.append((before, tile, after))
        outs = []
        for z in range(2):
            out = shifted[z + 1][1]
            for b in range(3):
                acc = None
                for a in range(3):
                    for c in range(3):
                        term = cpl[z, 9 * b + 3 * a + c] * shifted[z + a][c]
                        acc = term if acc is None else acc + term
                if b != 1:
                    acc = pltpu.roll(acc, (1 - b) % 8, 0)
                out = out + acc
            outs.append(out)
        return outs

    y_wait(0)
    for c in range(CHUNKS):
        z_wait(0, c)
        edges = arrived(0)

        def first(step, packs, c=c, edges=edges):
            packs = list(packs)
            for u in range(2):
                k = c * per + step * 2 + u
                outs = step_column(f0, k, edges)
                for z in range(2):
                    f1[1 + z, k] = outs[z]
                    packs[z] = pack_into(packs[z], outs[z], k)
            return tuple(packs)

        packs = lax.fori_loop(0, per // 2, first, (zero_tile, zero_tile))
        for z in range(2):
            ysend[1 + c, z] = packs[z]
        y_start(1 + c)
        z_start(1, c)

    for c in range(CHUNKS):
        y_wait(1 + c)
        z_wait(1, c)
        edges = arrived(1 + c)

        def second(step, carry, c=c, edges=edges):
            for u in range(2):
                k = c * per + step * 2 + u
                outs = step_column(f1, k, edges)
                for z in range(2):
                    x2[z, pl.ds(pl.multiple_of(k * 8, 8), 8), :] = outs[z]
            return carry

        lax.fori_loop(0, per // 2, second, 0)

    for z in range(2):
        for x in range(8):
            piece = x2[z, pl.ds(x, cols, stride=8), :]
            at = (z * 8 + x) * 128
            high = piece.astype(jnp.bfloat16)
            rest = piece - high.astype(jnp.float32)
            mid = rest.astype(jnp.bfloat16)
            low = (rest - mid.astype(jnp.float32)).astype(jnp.bfloat16)
            xs[0:cols, at : at + 128] = high
            xs[cols : 2 * cols, at : at + 128] = mid
            xs[2 * cols : 3 * cols, at : at + 128] = low

    products = lax.dot_general(
        xs[...], xs[...], (((1,), (1,)), ((), ())), preferred_element_type=jnp.float32
    )
    rows = products[0:cols] + (products[cols : 2 * cols] + products[2 * cols :])
    gram = rows[:, 0:cols] + (rows[:, cols : 2 * cols] + rows[:, 2 * cols :])
    half = cols // 2
    packed = jnp.concatenate([gram[0:half], gram[half:]], axis=1)

    def exchange(buf, me, n, partner, send, recv, value):
        buf[me] = value
        copies = []
        for off in range(1, n):
            _, dev = partner(off)
            copy = pltpu.make_async_remote_copy(
                src_ref=buf.at[me], dst_ref=buf.at[me],
                send_sem=send.at[off], recv_sem=recv.at[me],
                device_id=dev, device_id_type=MESH,
            )
            copy.start()
            copies.append(copy)
        for off in range(1, n):
            other, dev = partner(off)
            pltpu.make_async_remote_copy(
                src_ref=buf.at[other], dst_ref=buf.at[other],
                send_sem=send.at[off], recv_sem=recv.at[other],
                device_id=dev, device_id_type=MESH,
            ).wait_recv()
        out = buf[0]
        for i in range(1, n):
            out = out + buf[i]
        return out, copies

    packed, sent_a = exchange(buf_a, me_a, n_a, partner_a, a_send, a_recv, packed)
    packed, sent_b = exchange(buf_b, outer, so, partner_b, b_send, b_recv, packed)

    blocks = cols // 8
    tiles = []
    for i in range(blocks):
        if i * 8 < half:
            tile = packed[i * 8 : i * 8 + 8]
        else:
            at = i * 8 - half
            tile = pltpu.roll(packed[at : at + 8], 64, 1)
        unit = jnp.where(lane - cols == sub + 8 * i, 1.0, 0.0)
        tiles.append(jnp.where(lane < cols, tile, unit))
    pivots = [zero_tile] * blocks
    for k in range(cols):
        own, r = k // 8, k % 8
        row = jnp.broadcast_to(tiles[own][r : r + 1, :], (8, 128))
        column = jnp.broadcast_to(tiles[own][:, k : k + 1], (8, 128))
        pivot = jnp.broadcast_to(column[r : r + 1, :], (8, 128))
        pivots[own] = jnp.where(sub == r, pivot, pivots[own])
        scaled = row * (1.0 / pivot)
        for i in range(own, blocks):
            if i > own:
                column = jnp.broadcast_to(tiles[i][:, k : k + 1], (8, 128))
            elif r == 7:
                continue
            else:
                column = jnp.where(sub > r, column, 0.0)
            tiles[i] = tiles[i] - column * scaled

    root = jnp.float32(cells) ** 0.5
    weights = []
    for i in range(blocks):
        scale = 1.0 / jnp.sqrt(pivots[i])
        tile = tiles[i] * scale
        upper = jnp.where(lane >= sub + 8 * i, tile, 0.0) / root
        r_out[8 * i : 8 * i + 8, :] = upper[:, 0:cols]
        weights.append(pltpu.roll(tile, 64, 1)[:, 0:cols] * root)
    weight = jnp.concatenate(weights, axis=0)
    high = weight.astype(jnp.bfloat16)
    rest = weight - high.astype(jnp.float32)
    mid = rest.astype(jnp.bfloat16)
    low = (rest - mid.astype(jnp.float32)).astype(jnp.bfloat16)
    stacked = jnp.concatenate([jnp.concatenate([w] * 3, axis=1) for w in (high, mid, low)], axis=0)
    for z in range(2):
        for x in range(0, 8, 2):
            at = (z * 8 + x) * 128
            got = jnp.dot(stacked, xs[:, at : at + 256], preferred_element_type=jnp.float32)
            got = got[0:cols] + (got[cols : 2 * cols] + got[2 * cols :])
            for u in range(2):
                x2[z, pl.ds(x + u, cols, stride=8), :] = got[:, u * 128 : u * 128 + 128]
    for z in range(2):
        q_out[:, z] = x2[z].reshape(cols, 8, 128)

    for e in range(2):
        for c in range(CHUNKS):
            for way, present in ((0, has_lo), (1, has_hi)):
                @pl.when(present)
                def _(e=e, c=c, way=way):
                    z_copy(e, c, way).wait_send()
    for slot in range(CHUNKS + 1):
        for d in range(n_dir):
            y_copy(slot, d, 0).wait_send()
            for which, present in ((1, has_lo), (2, has_hi)):
                @pl.when(present)
                def _(slot=slot, d=d, which=which):
                    y_copy(slot, d, which).wait_send()
    for copy in sent_a + sent_b:
        copy.wait_send()


def solution(mesh):
    n_zn, n_zw = mesh.shape["zn"], mesh.shape["zw"]

    def on_device(basis, coupling):
        cols, planes, nx, span = basis.shape
        si = inner_size(n_zw)
        so = n_zw // si
        n_a = n_zn * si
        n_dir = 1 if n_zn == 2 else 2
        f32 = jnp.float32
        dma = pltpu.SemaphoreType.DMA
        cells = planes * nx * span * n_zn * n_zw
        return pl.pallas_call(
            functools.partial(kernel, n_zn, n_zw, cells),
            out_shape=(
                jax.ShapeDtypeStruct(basis.shape, f32),
                jax.ShapeDtypeStruct((cols, cols), f32),
            ),
            in_specs=[pl.BlockSpec(memory_space=pl.ANY), pl.BlockSpec(memory_space=pltpu.VMEM)],
            out_specs=(
                pl.BlockSpec(memory_space=pltpu.VMEM),
                pl.BlockSpec(memory_space=pltpu.VMEM),
            ),
            scratch_shapes=[
                pltpu.VMEM((4, cols, nx, span), f32),
                pltpu.VMEM((4, cols, nx, span), f32),
                pltpu.VMEM((planes, cols * nx, span), f32),
                pltpu.VMEM((planes, 27, nx, span), f32),
                pltpu.VMEM((CHUNKS + 1, 2, nx, span), f32),
                pltpu.VMEM((n_dir, CHUNKS + 1, 4, nx, span), f32),
                pltpu.VMEM((3 * cols, planes * nx * span), jnp.bfloat16),
                pltpu.VMEM((n_a, cols // 2, 2 * cols), f32),
                pltpu.VMEM((so, cols // 2, 2 * cols), f32),
                dma((2,)),
                dma((2, CHUNKS, 2)),
                dma((2, CHUNKS, 2)),
                dma((CHUNKS + 1, n_dir, 3)),
                dma((CHUNKS + 1, n_dir, 3)),
                dma((n_a,)),
                dma((n_a,)),
                dma((so,)),
                dma((so,)),
            ],
            compiler_params=pltpu.CompilerParams(
                collective_id=0, has_side_effects=True, vmem_limit_bytes=32 * 1024 * 1024
            ),
        )(basis, coupling)

    spec = P(None, "zw", None, "zn")
    return jax.shard_map(
        on_device, mesh=mesh, in_specs=(spec, spec), out_specs=(spec, P()), check_vma=False
    )
```

time: 344 us -> 45.8 us (0.13)
  matrix products: 102 us -> 0 us
  other arithmetic: 65.1 us -> 0 us
  blocking collectives: 49 us -> 0 us
  loops' own time: 47.8 us -> 0 us
  Pallas kernels: 0 us -> 41.6 us
  local copies, waits for them, and re-layouts: 44.8 us -> 3.34 us
  starting transfers between devices: 18.9 us -> 0 us
  waiting for transfers between devices: 11.9 us -> 0 us
    dot_general x130 -> x0, matrix products: 102 us -> none  [the longest x64 50 us: one_row(): jnp.dot(above, inverse, precision=lax.Precision.HIGHEST)]
    psum x1 -> x0, blocking collectives: 49 us -> none  [on_device(): gram_matrix = lax.psum(inner_products(flat_basis), ('zn', 'zw'))]
    another operation x2 -> x0, loops' own time: 47.8 us -> none  [the longest x1 46.3 us: upper_cholesky(): return lax.fori_loop(0, order, one_row, jnp.zeros_like(gram_matrix))]
    pallas_call x0 -> x1, Pallas kernels: none -> 41.6 us  [on_device(): pl.pallas_call(functools.partial(kernel, n_zn, n_zw, cells), out_shape=(j...]
    reduce_sum x64 -> x0, other arithmetic: 38.8 us -> none  [one_row(): pivot = jnp.sum(jnp.where(places == index, row, 0.0))]
    mul x27 -> x0, local copies, waits for them, and re-layouts: 19.3 us -> none  [sweep(): summed = summed + coupling[offset].astype(jnp.float32)[None] * source]
    ppermute x8 -> x0, starting transfers between devices: 18.9 us -> none  [the longest x4 15.2 us: with_halo(): before = lax.ppermute(last, axis, up)]
    add x2 -> x0, other arithmetic: 18.1 us -> none  [sweep(): summed = summed + coupling[offset].astype(jnp.float32)[None] * source]
  transfers between devices with their start and end apart: 8 -> 0, of which waited for: 5 -> 0; matrix products, arithmetic and copies ran while one was open for 6% -> 0% of each run, Pallas kernels for 0% -> 0%
where the time goes in v1:
time: 45.8 us; the launch traced here: 45.6 us
  Pallas kernels  41.6 us (91%)
  local copies, waits for them, and re-layouts  3.34 us (7%)
  between operations  0.65 us (1%)
    pallas_call x1, Pallas kernels, on_device(): pl.pallas_call(functools.partial(kernel, n_zn, n_zw, cells), out_shape=(j...  41.6 us
    unnamed x6, local copies, waits for them, and re-layouts  3.34 us

profile of v1, /device:TPU:0, one launch (start us, length us, event | category | flops | bytes accessed | tf_op | source)
XLA Modules:
  0.0 45.6 jit_solution(8037991242647816736)
XLA Ops:
  0.6 0.0 copy-start
  0.6 1.0 %copy-done = f32[64,2,8,128]{3,2,1,0:T(8,128)S(1)} copy-done((f32[64,2,8,128]{3,2,1,0:T(8,128)S(1)}, f32[64,2,8,128]{3,2,1,0:T(8,128)}, u32[]{:S(2)}) %copy-start) | copy-done | bytes 524312
  1.7 0.0 copy-start.1
  1.7 0.9 %copy-done.1 = bf16[27,2,8,128]{3,2,1,0:T(8,128)(2,1)S(1)} copy-done((bf16[27,2,8,128]{3,2,1,0:T(8,128)(2,1)S(1)}, bf16[27,2,8,128]{3,2,1,0:T(8,128)(2,1)}, u32[]{:S(2)}) %copy-start.1) | copy-done | bytes 110616
  2.6 41.6 %shard_map.41 = (f32[64,2,8,128]{3,2,1,0:T(8,128)S(1)}, f32[64,64]{1,0:T(8,128)S(1)}) custom-call(f32[64,2,8,128]{3,2,1,0:T(8,128)S(1)} %copy-done, bf16[27,2,8,128]{3,2,1,0:T(8,128)(2,1)S(1)} %copy-done.1), custom_call_target="tpu_custom_call" | custom-call | tf_op jit(solution)/shard_map/pallas_call | solution.py:371
  44.2 0.8 %copy.6 = f32[64,2,8,128]{3,2,1,0:T(8,128)} copy(f32[64,2,8,128]{3,2,1,0:T(8,128)S(1)} %get-tuple-element.4) | data formatting | bytes 1048576
  45.0 0.6 %copy.7 = f32[64,64]{1,0:T(8,128)} copy(f32[64,64]{1,0:T(8,128)S(1)} %get-tuple-element.5) | data formatting | bytes 32768
Async XLA Ops:
  0.6 1.0 %copy-start = (f32[64,2,8,128]{3,2,1,0:T(8,128)S(1)}, f32[64,2,8,128]{3,2,1,0:T(8,128)}, u32[]{:S(2)}) copy-start(f32[64,2,8,128]{3,2,1,0:T(8,128)} %basis.1) | copy-start | bytes 1572868
  1.7 0.9 %copy-start.1 = (bf16[27,2,8,128]{3,2,1,0:T(8,128)(2,1)S(1)}, bf16[27,2,8,128]{3,2,1,0:T(8,128)(2,1)}, u32[]{:S(2)}) copy-start(bf16[27,2,8,128]{3,2,1,0:T(8,128)(2,1)} %coupling.1) | copy-start | bytes 331780

commit v2 on v1

--- a/solution.py
+++ b/solution.py
@@ -85,8 +85,8 @@
             f0[plane] = jnp.zeros(f0.shape[1:], jnp.float32)
             f1[plane] = jnp.zeros(f1.shape[1:], jnp.float32)
             for d in range(n_dir):
-                for c in range(CHUNKS + 1):
-                    yrecv[d, c, plane] = zero_tile
+                for e in range(2):
+                    yrecv[d, e, plane] = jnp.zeros(yrecv.shape[3:], jnp.float32)
 
     total = (n_a - 1) + (so - 1)
     both = has_lo.astype(jnp.int32) + has_hi.astype(jnp.int32)
@@ -117,30 +117,34 @@
             def _(way=way):
                 z_copy(e, c, way).wait_recv()
 
-    def y_copy(slot, d, which):
+    def y_copy(e, c, d, which):
         dz, src, dst = ((0, (0, 2), 1), (-1, (0, 1), 3), (1, (1, 1), 0))[which]
+        if c is None:
+            part, at = slice(None), CHUNKS
+        else:
+            part, at = pl.ds(c, 1), c
         return pltpu.make_async_remote_copy(
-            src_ref=ysend.at[slot, pl.ds(src[0], src[1])],
-            dst_ref=yrecv.at[d, slot, pl.ds(dst, src[1])],
-            send_sem=y_send.at[slot, d, which], recv_sem=y_recv.at[slot, d, which],
+            src_ref=ysend.at[e, pl.ds(src[0], src[1]), part],
+            dst_ref=yrecv.at[d, e, pl.ds(dst, src[1]), part],
+            send_sem=y_send.at[at, d, which], recv_sem=y_recv.at[at, d, which],
             device_id={"zn": beside(sides[d]), "zw": zw + dz}, device_id_type=MESH,
         )
 
-    def y_start(slot):
+    def y_start(e, c):
         for d in range(n_dir):
-            y_copy(slot, d, 0).start()
+            y_copy(e, c, d, 0).start()
             for which, present in ((1, has_lo), (2, has_hi)):
                 @pl.when(present)
                 def _(d=d, which=which):
-                    y_copy(slot, d, which).start()
-
-    def y_wait(slot):
+                    y_copy(e, c, d, which).start()
+
+    def y_wait(e, c):
         for d in range(n_dir):
-            y_copy(slot, d, 0).wait_recv()
+            y_copy(e, c, d, 0).wait_recv()
             for which, present in ((1, has_hi), (2, has_lo)):
                 @pl.when(present)
                 def _(d=d, which=which):
-                    y_copy(slot, d, which).wait_recv()
+                    y_copy(e, c, d, which).wait_recv()
 
     for c in range(CHUNKS):
         z_start(0, c)
@@ -148,21 +152,20 @@
     for copy in loads:
         copy.wait()
 
-    def pack_into(packed, tile, k):
-        return jnp.where(pair == k, pltpu.roll(tile, 2 * k + 1, 1), packed)
-
-    def pack_first(step, packs):
-        packs = list(packs)
-        for u in range(4):
-            k = step * 4 + u
+    def pack_into(packed, tile, u):
+        return jnp.where(pair == u, pltpu.roll(tile, 2 * u + 1, 1), packed)
+
+    def pack_first(c, carry):
+        packs = [zero_tile, zero_tile]
+        for u in range(per):
             for z in range(2):
-                packs[z] = pack_into(packs[z], f0[1 + z, k], k)
-        return tuple(packs)
-
-    packs = lax.fori_loop(0, cols // 4, pack_first, (zero_tile, zero_tile))
-    for z in range(2):
-        ysend[0, z] = packs[z]
-    y_start(0)
+                packs[z] = pack_into(packs[z], f0[1 + z, c * per + u], u)
+        for z in range(2):
+            ysend[0, z, c] = packs[z]
+        return carry
+
+    lax.fori_loop(0, CHUNKS, pack_first, 0)
+    y_start(0, None)
 
     for z in range(2):
         for b in range(3):
@@ -173,20 +176,20 @@
                         tile = pltpu.roll(tile, (b - 1) % 8, 0)
                     cpl[z, 9 * b + 3 * a + c] = tile
 
-    def arrived(slot):
+    def arrived(e, c):
         result = []
         for plane in range(4):
-            tile = yrecv[0, slot, plane]
+            tile = yrecv[0, e, plane, c]
             if n_dir == 2:
-                tile = jnp.where(lane % 2 == 0, tile, yrecv[1, slot, plane])
+                tile = jnp.where(lane % 2 == 0, tile, yrecv[1, e, plane, c])
             result.append(tile)
         return result
 
-    def step_column(f, k, edges):
+    def step_column(f, k, u, edges):
         shifted = []
         for plane in range(4):
             tile = f[plane, k]
-            edge = pltpu.roll(edges[plane], 127 - 2 * k, 1)
+            edge = pltpu.roll(edges[plane], 127 - 2 * u, 1)
             before = pltpu.roll(jnp.where(lane == 127, edge, tile), 1, 1)
             after = pltpu.roll(jnp.where(lane == 0, edge, tile), 127, 1)
             shifted.append((before, tile, after))
@@ -205,41 +208,36 @@
             outs.append(out)
         return outs
 
-    y_wait(0)
-    for c in range(CHUNKS):
+    def first(c, carry):
         z_wait(0, c)
-        edges = arrived(0)
-
-        def first(step, packs, c=c, edges=edges):
-            packs = list(packs)
-            for u in range(2):
-                k = c * per + step * 2 + u
-                outs = step_column(f0, k, edges)
-                for z in range(2):
-                    f1[1 + z, k] = outs[z]
-                    packs[z] = pack_into(packs[z], outs[z], k)
-            return tuple(packs)
-
-        packs = lax.fori_loop(0, per // 2, first, (zero_tile, zero_tile))
+        edges = arrived(0, c)
+        packs = [zero_tile, zero_tile]
+        for u in range(per):
+            k = c * per + u
+            outs = step_column(f0, k, u, edges)
+            for z in range(2):
+                f1[1 + z, k] = outs[z]
+                packs[z] = pack_into(packs[z], outs[z], u)
         for z in range(2):
-            ysend[1 + c, z] = packs[z]
-        y_start(1 + c)
+            ysend[1, z, c] = packs[z]
         z_start(1, c)
-
-    for c in range(CHUNKS):
-        y_wait(1 + c)
+        y_start(1, c)
+        return carry
+
+    def second(c, carry):
+        y_wait(1, c)
         z_wait(1, c)
-        edges = arrived(1 + c)
-
-        def second(step, carry, c=c, edges=edges):
-            for u in range(2):
-                k = c * per + step * 2 + u
-                outs = step_column(f1, k, edges)
-                for z in range(2):
-                    x2[z, pl.ds(pl.multiple_of(k * 8, 8), 8), :] = outs[z]
-            return carry
-
-        lax.fori_loop(0, per // 2, second, 0)
+        edges = arrived(1, c)
+        for u in range(per):
+            k = c * per + u
+            outs = step_column(f1, k, u, edges)
+            for z in range(2):
+                x2[z, pl.ds(pl.multiple_of(k * 8, 8), 8), :] = outs[z]
+        return carry
+
+    y_wait(0, None)
+    lax.fori_loop(0, CHUNKS, first, 0)
+    lax.fori_loop(0, CHUNKS, second, 0)
 
     for z in range(2):
         for x in range(8):
@@ -298,22 +296,50 @@
             tile = pltpu.roll(packed[at : at + 8], 64, 1)
         unit = jnp.where(lane - cols == sub + 8 * i, 1.0, 0.0)
         tiles.append(jnp.where(lane < cols, tile, unit))
-    pivots = [zero_tile] * blocks
-    for k in range(cols):
-        own, r = k // 8, k % 8
-        row = jnp.broadcast_to(tiles[own][r : r + 1, :], (8, 128))
-        column = jnp.broadcast_to(tiles[own][:, k : k + 1], (8, 128))
-        pivot = jnp.broadcast_to(column[r : r + 1, :], (8, 128))
-        pivots[own] = jnp.where(sub == r, pivot, pivots[own])
-        scaled = row * (1.0 / pivot)
-        for i in range(own, blocks):
-            if i > own:
-                column = jnp.broadcast_to(tiles[i][:, k : k + 1], (8, 128))
-            elif r == 7:
-                continue
-            else:
-                column = jnp.where(sub > r, column, 0.0)
-            tiles[i] = tiles[i] - column * scaled
+    sums = [zero_tile] * blocks
+    pivots = []
+    for own in range(blocks):
+        base = own * 8
+        now = [tiles[i] - sums[i] for i in range(own, blocks)]
+        columns = [
+            [jnp.broadcast_to(tile[:, base + s : base + s + 1], (8, 128)) for s in range(8)]
+            for tile in now
+        ]
+        block = [
+            [jnp.broadcast_to(columns[0][s][t : t + 1, :], (8, 128)) for s in range(8)]
+            for t in range(8)
+        ]
+        rows = [jnp.broadcast_to(now[0][s : s + 1, :], (8, 128)) for s in range(8)]
+        done, pivot_tile = zero_tile, zero_tile
+        add_block, add_rows = {}, {}
+        add_columns = [dict() for _ in now]
+
+        def plus(table, key, value):
+            table[key] = table[key] + value if key in table else value
+
+        def less(table, key, value):
+            return value - table[key] if key in table else value
+
+        for s in range(8):
+            pivot = less(add_block, (s, s), block[s][s])
+            inverse = 1.0 / pivot
+            row = less(add_rows, s, rows[s])
+            scaled = row * inverse
+            done = jnp.where(sub == s, row, done)
+            pivot_tile = jnp.where(sub == s, pivot, pivot_tile)
+            entries = {t: less(add_block, (s, t), block[s][t]) for t in range(s + 1, 8)}
+            factors = {t: entries[t] * inverse for t in entries}
+            for t in entries:
+                for v in range(t, 8):
+                    plus(add_block, (t, v), entries[t] * factors[v])
+                plus(add_rows, t, entries[t] * scaled)
+            for j in range(1, len(now)):
+                column = less(add_columns[j], s, columns[j][s])
+                for t in entries:
+                    plus(add_columns[j], t, column * factors[t])
+                sums[own + j] = sums[own + j] + column * scaled
+        tiles[own] = done
+        pivots.append(pivot_tile)
 
     root = jnp.float32(cells) ** 0.5
     weights = []
@@ -345,13 +371,13 @@
                 @pl.when(present)
                 def _(e=e, c=c, way=way):
                     z_copy(e, c, way).wait_send()
-    for slot in range(CHUNKS + 1):
+    for e, c in [(0, None)] + [(1, c) for c in range(CHUNKS)]:
         for d in range(n_dir):
-            y_copy(slot, d, 0).wait_send()
+            y_copy(e, c, d, 0).wait_send()
             for which, present in ((1, has_lo), (2, has_hi)):
                 @pl.when(present)
-                def _(slot=slot, d=d, which=which):
-                    y_copy(slot, d, which).wait_send()
+                def _(e=e, c=c, d=d, which=which):
+                    y_copy(e, c, d, which).wait_send()
     for copy in sent_a + sent_b:
         copy.wait_send()
 
@@ -384,8 +410,8 @@
                 pltpu.VMEM((4, cols, nx, span), f32),
                 pltpu.VMEM((planes, cols * nx, span), f32),
                 pltpu.VMEM((planes, 27, nx, span), f32),
-                pltpu.VMEM((CHUNKS + 1, 2, nx, span), f32),
-                pltpu.VMEM((n_dir, CHUNKS + 1, 4, nx, span), f32),
+                pltpu.VMEM((2, 2, CHUNKS, nx, span), f32),
+                pltpu.VMEM((n_dir, 2, 4, CHUNKS, nx, span), f32),
                 pltpu.VMEM((3 * cols, planes * nx * span), jnp.bfloat16),
                 pltpu.VMEM((n_a, cols // 2, 2 * cols), f32),
                 pltpu.VMEM((so, cols // 2, 2 * cols), f32),

time: 45.8 us -> 37.5 us (0.82)
  Pallas kernels: 41.6 us -> 33.3 us
    pallas_call x1, Pallas kernels: 41.6 us -> 33.3 us  [on_device(): pl.pallas_call(functools.partial(kernel, n_zn, n_zw, cells), out_shape=(j...]
where the time goes in v2:
time: 37.5 us; the launch traced here: 37.3 us
  Pallas kernels  33.3 us (89%)
  local copies, waits for them, and re-layouts  3.34 us (9%)
  between operations  0.65 us (2%)
    pallas_call x1, Pallas kernels, on_device(): pl.pallas_call(functools.partial(kernel, n_zn, n_zw, cells), out_shape=(j...  33.3 us
    unnamed x6, local copies, waits for them, and re-layouts  3.34 us

profile of v2, /device:TPU:0, one launch (start us, length us, event | category | flops | bytes accessed | tf_op | source)
XLA Modules:
  0.0 37.3 jit_solution(17280692149006134612)
XLA Ops:
  0.6 0.0 copy-start
  0.6 1.0 %copy-done = f32[64,2,8,128]{3,2,1,0:T(8,128)S(1)} copy-done((f32[64,2,8,128]{3,2,1,0:T(8,128)S(1)}, f32[64,2,8,128]{3,2,1,0:T(8,128)}, u32[]{:S(2)}) %copy-start) | copy-done | bytes 524312
  1.7 0.0 copy-start.1
  1.7 0.9 %copy-done.1 = bf16[27,2,8,128]{3,2,1,0:T(8,128)(2,1)S(1)} copy-done((bf16[27,2,8,128]{3,2,1,0:T(8,128)(2,1)S(1)}, bf16[27,2,8,128]{3,2,1,0:T(8,128)(2,1)}, u32[]{:S(2)}) %copy-start.1) | copy-done | bytes 110616
  2.6 33.3 %shard_map.41 = (f32[64,2,8,128]{3,2,1,0:T(8,128)S(1)}, f32[64,64]{1,0:T(8,128)S(1)}) custom-call(f32[64,2,8,128]{3,2,1,0:T(8,128)S(1)} %copy-done, bf16[27,2,8,128]{3,2,1,0:T(8,128)(2,1)S(1)} %copy-done.1), custom_call_target="tpu_custom_call" | custom-call | tf_op jit(solution)/shard_map/pallas_call | solution.py:397
  35.9 0.8 %copy.6 = f32[64,2,8,128]{3,2,1,0:T(8,128)} copy(f32[64,2,8,128]{3,2,1,0:T(8,128)S(1)} %get-tuple-element.4) | data formatting | bytes 1048576
  36.7 0.6 %copy.7 = f32[64,64]{1,0:T(8,128)} copy(f32[64,64]{1,0:T(8,128)S(1)} %get-tuple-element.5) | data formatting | bytes 32768
Async XLA Ops:
  0.6 1.0 %copy-start = (f32[64,2,8,128]{3,2,1,0:T(8,128)S(1)}, f32[64,2,8,128]{3,2,1,0:T(8,128)}, u32[]{:S(2)}) copy-start(f32[64,2,8,128]{3,2,1,0:T(8,128)} %basis.1) | copy-start | bytes 1572868
  1.7 0.9 %copy-start.1 = (bf16[27,2,8,128]{3,2,1,0:T(8,128)(2,1)S(1)}, bf16[27,2,8,128]{3,2,1,0:T(8,128)(2,1)}, u32[]{:S(2)}) copy-start(bf16[27,2,8,128]{3,2,1,0:T(8,128)(2,1)} %coupling.1) | copy-start | bytes 331780

commit v3 on v2

--- a/solution.py
+++ b/solution.py
@@ -8,7 +8,7 @@
 from jax.sharding import PartitionSpec as P
 
 MESH = pl.DeviceIdType.MESH
-CHUNKS = 4
+CHUNKS = 8
 
 
 def inner_size(n):
@@ -21,8 +21,8 @@
 
 
 def kernel(
-    n_zn, n_zw, cells, basis, coupling, q_out, r_out,
-    f0, f1, x2, cpl, ysend, yrecv, xs, buf_a, buf_b,
+    n_zn, n_zw, cells, basis, coupling_far, q_out, r_out,
+    coupling, f0, f1, x2, cpl, ysend, yrecv, xs, buf_a, buf_b,
     load_sem, z_send, z_recv, y_send, y_recv, a_send, a_recv, b_send, b_recv,
 ):
     zn = lax.axis_index("zn")
@@ -71,8 +71,10 @@
     loads = [
         pltpu.make_async_copy(basis.at[:, z], f0.at[1 + z], load_sem.at[z]) for z in range(2)
     ]
+    load_coupling = pltpu.make_async_copy(coupling_far, coupling, load_sem.at[2])
     for copy in loads:
         copy.start()
+    load_coupling.start()
 
     lane = lax.broadcasted_iota(jnp.int32, (8, 128), 1)
     sub = lax.broadcasted_iota(jnp.int32, (8, 128), 0)
@@ -146,7 +148,7 @@
                 def _(d=d, which=which):
                     y_copy(e, c, d, which).wait_recv()
 
-    for c in range(CHUNKS):
+    for c in range(CHUNKS // 2):
         z_start(0, c)
 
     for copy in loads:
@@ -166,7 +168,10 @@
 
     lax.fori_loop(0, CHUNKS, pack_first, 0)
     y_start(0, None)
-
+    for c in range(CHUNKS // 2, CHUNKS):
+        z_start(0, c)
+
+    load_coupling.wait()
     for z in range(2):
         for b in range(3):
             for a in range(3):
@@ -220,8 +225,8 @@
                 packs[z] = pack_into(packs[z], outs[z], u)
         for z in range(2):
             ysend[1, z, c] = packs[z]
+        y_start(1, c)
         z_start(1, c)
-        y_start(1, c)
         return carry
 
     def second(c, carry):
@@ -400,12 +405,13 @@
                 jax.ShapeDtypeStruct(basis.shape, f32),
                 jax.ShapeDtypeStruct((cols, cols), f32),
             ),
-            in_specs=[pl.BlockSpec(memory_space=pl.ANY), pl.BlockSpec(memory_space=pltpu.VMEM)],
+            in_specs=[pl.BlockSpec(memory_space=pltpu.HBM)] * 2,
             out_specs=(
                 pl.BlockSpec(memory_space=pltpu.VMEM),
                 pl.BlockSpec(memory_space=pltpu.VMEM),
             ),
             scratch_shapes=[
+                pltpu.VMEM(coupling.shape, coupling.dtype),
                 pltpu.VMEM((4, cols, nx, span), f32),
                 pltpu.VMEM((4, cols, nx, span), f32),
                 pltpu.VMEM((planes, cols * nx, span), f32),
@@ -415,7 +421,7 @@
                 pltpu.VMEM((3 * cols, planes * nx * span), jnp.bfloat16),
                 pltpu.VMEM((n_a, cols // 2, 2 * cols), f32),
                 pltpu.VMEM((so, cols // 2, 2 * cols), f32),
-                dma((2,)),
+                dma((3,)),
                 dma((2, CHUNKS, 2)),
                 dma((2, CHUNKS, 2)),
                 dma((CHUNKS + 1, n_dir, 3)),

time: 37.5 us -> 36.4 us (0.971)
  Pallas kernels: 33.3 us -> 32.2 us
    pallas_call x1, Pallas kernels: 33.3 us -> 32.2 us  [on_device(): pl.pallas_call(functools.partial(kernel, n_zn, n_zw, cells), out_shape=(j...]
where the time goes in v3:
time: 36.4 us; the launch traced here: 36.2 us
  Pallas kernels  32.2 us (88%)
  local copies, waits for them, and re-layouts  3.34 us (9%)
  between operations  0.65 us (2%)
    pallas_call x1, Pallas kernels, on_device(): pl.pallas_call(functools.partial(kernel, n_zn, n_zw, cells), out_shape=(j...  32.2 us
    unnamed x6, local copies, waits for them, and re-layouts  3.34 us

profile of v3, /device:TPU:0, one launch (start us, length us, event | category | flops | bytes accessed | tf_op | source)
XLA Modules:
  0.0 36.2 jit_solution(5466343026320918086)
XLA Ops:
  0.6 0.0 copy-start
  0.6 1.0 %copy-done = f32[64,2,8,128]{3,2,1,0:T(8,128)S(1)} copy-done((f32[64,2,8,128]{3,2,1,0:T(8,128)S(1)}, f32[64,2,8,128]{3,2,1,0:T(8,128)}, u32[]{:S(2)}) %copy-start) | copy-done | bytes 524312
  1.7 0.0 copy-start.1
  1.7 0.9 %copy-done.1 = bf16[27,2,8,128]{3,2,1,0:T(8,128)(2,1)S(1)} copy-done((bf16[27,2,8,128]{3,2,1,0:T(8,128)(2,1)S(1)}, bf16[27,2,8,128]{3,2,1,0:T(8,128)(2,1)}, u32[]{:S(2)}) %copy-start.1) | copy-done | bytes 110616
  2.6 32.2 %shard_map.41 = (f32[64,2,8,128]{3,2,1,0:T(8,128)S(1)}, f32[64,64]{1,0:T(8,128)S(1)}) custom-call(f32[64,2,8,128]{3,2,1,0:T(8,128)S(1)} %copy-done, bf16[27,2,8,128]{3,2,1,0:T(8,128)(2,1)S(1)} %copy-done.1), custom_call_target="tpu_custom_call" | custom-call | tf_op jit(solution)/shard_map/pallas_call | solution.py:402
  34.8 0.8 %copy.6 = f32[64,2,8,128]{3,2,1,0:T(8,128)} copy(f32[64,2,8,128]{3,2,1,0:T(8,128)S(1)} %get-tuple-element.4) | data formatting | bytes 1048576
  35.6 0.6 %copy.7 = f32[64,64]{1,0:T(8,128)} copy(f32[64,64]{1,0:T(8,128)S(1)} %get-tuple-element.5) | data formatting | bytes 32768
Async XLA Ops:
  0.6 1.0 %copy-start = (f32[64,2,8,128]{3,2,1,0:T(8,128)S(1)}, f32[64,2,8,128]{3,2,1,0:T(8,128)}, u32[]{:S(2)}) copy-start(f32[64,2,8,128]{3,2,1,0:T(8,128)} %basis.1) | copy-start | bytes 1572868
  1.7 0.9 %copy-start.1 = (bf16[27,2,8,128]{3,2,1,0:T(8,128)(2,1)S(1)}, bf16[27,2,8,128]{3,2,1,0:T(8,128)(2,1)}, u32[]{:S(2)}) copy-start(bf16[27,2,8,128]{3,2,1,0:T(8,128)(2,1)} %coupling_far.1) | copy-start | bytes 331780
